TPU v7x, 512 devices: a whole 4x8x8 slice. The times are simulated.
512 devices in a mesh: seq: 64 (over z, x, core), head: 8 (over y).
Axes of the slice: x: 4, y: 8, z: 8, core: 2. Of those that a mesh axis runs over, the one named last changes fastest.
Arguments:
- queries: bfloat16 [24576, 4096], P('seq', 'head'), may hold values from -8 to 8
- keys: bfloat16 [24576, 4096], P('seq', 'head'), may hold values from -8 to 8
- values: bfloat16 [24576, 4096], P('seq', 'head'), may hold values from -6 to 6
- target_row: int32 [24576], P('seq'), may hold values from 0 to 24575, as said below
- doc_lengths: int32 [128], replicated, may hold values from 0 to 768, as said below
Outputs:
- mixed: bfloat16 [24576, 4096], P('seq', 'head')
Inputs may be any that keep to these rules, and one draw needn't show every extreme that they name: `target_row`: A permutation of the rows. The rows of one device go to at most 9 rows of any one device's block of 384 rows in document order, and every device sends exactly 9 rows to some device. `doc_lengths`: they sum to 24576; zero lengths occur; no document crosses a multiple of 768 rows, and some document fills the rows between two such multiples.
All inputs are finite; a program needn't handle non-finite values.
Results may differ from a plain program's by a relative error of at most 0.0035.
Values may be sent and summed in bfloat16 or wider, within the bound.
A program may use at most 64 MiB of HBM per device.

v0:
```python
import math

import jax
import jax.numpy as jnp
from jax import lax
from jax.sharding import PartitionSpec as P

HD = 128


block_rows = 512
neg_fill = -1e30


def swapped(block, axis, bit):
    count = lax.axis_size(axis)
    route = []
    for low in range(count):
        high = low | 1 << bit
        if high != low and high < count:
            route += [(low, high), (high, low)]
    return lax.ppermute(block, axis, route)


def attend(query_all, key_all, value_all, doc_lengths, first_row):
    length = query_all.shape[0]
    starts = jnp.cumsum(doc_lengths) - doc_lengths
    positions = first_row + jnp.arange(length, dtype=jnp.int32)
    labels = jnp.sum((starts[None, :] <= positions[:, None]).astype(jnp.int32), axis=1)
    scale = 1.0 / math.sqrt(query_all.shape[1])

    def one_block(index):
        start = index * block_rows
        query_block = lax.dynamic_slice_in_dim(query_all, start, block_rows, 0)
        label_block = lax.dynamic_slice_in_dim(labels, start, block_rows, 0)
        place_block = lax.dynamic_slice_in_dim(positions, start, block_rows, 0)
        scores = jnp.dot(query_block, key_all.T, preferred_element_type=jnp.float32) * scale
        allowed = (label_block[:, None] == labels[None, :]) & (
            positions[None, :] <= place_block[:, None]
        )
        scores = jnp.where(allowed, scores, neg_fill)
        top = jnp.max(scores, axis=1, keepdims=True)
        weights = jnp.where(allowed, jnp.exp(scores - top), 0.0)
        total = jnp.sum(weights, axis=1, keepdims=True)
        mixed = (
            jnp.dot(weights.astype(jnp.bfloat16), value_all, preferred_element_type=jnp.float32)
            / total
        )
        return mixed.astype(jnp.bfloat16)

    result = lax.map(one_block, jnp.arange(length // block_rows, dtype=jnp.int32))
    return result.reshape(length, query_all.shape[1])


def body(queries, keys, values, target_row, doc_lengths):
    rows = queries.shape[0]
    width = queries.shape[1]
    group = width // HD
    devices = lax.axis_size("seq")
    capacity = 3 * rows // (2 * devices)
    bits = group.bit_length() - 1
    member = lax.axis_index("seq") % group
    first_row = lax.axis_index("seq") // group * (group * rows)
    target_device = target_row // rows
    target_local = target_row % rows
    stacked = jnp.stack([queries, keys, values])
    flags = (target_device[:, None] == jnp.arange(devices, dtype=jnp.int32)[None, :]).astype(
        jnp.int32
    )
    order = jnp.sum((jnp.cumsum(flags, axis=0) - flags) * flags, axis=1)
    slot = target_device * capacity + order
    outgoing = jnp.zeros((3, devices * capacity, width), jnp.bfloat16).at[:, slot].set(stacked)
    places = jnp.full((devices * capacity,), rows, jnp.int32).at[slot].set(target_local)
    incoming = lax.all_to_all(
        outgoing.reshape(3, devices, capacity, width),
        "seq",
        split_axis=1,
        concat_axis=1,
        tiled=True,
    )
    arrived = lax.all_to_all(
        places.reshape(devices, capacity), "seq", split_axis=0, concat_axis=0, tiled=True
    )
    placed = jnp.zeros((3, rows + 1, width), jnp.bfloat16)
    placed = placed.at[:, arrived.reshape(-1)].set(incoming.reshape(3, devices * capacity, width))[
        :, :rows
    ]
    state = jnp.transpose(placed.reshape(3, rows, group, HD), (0, 2, 1, 3)).reshape(
        (3,) + (2,) * bits + (rows, HD)
    )
    for step in range(bits):
        axis_pos = bits - step
        bit_value = member // 2**step % 2
        retained = lax.dynamic_index_in_dim(state, bit_value, axis_pos, keepdims=False)
        leaving = lax.dynamic_index_in_dim(state, 1 - bit_value, axis_pos, keepdims=False)
        received = swapped(leaving, "seq", step)
        state = jnp.where(
            bit_value == 0,
            jnp.stack([retained, received], axis_pos),
            jnp.stack([received, retained], axis_pos),
        )
    packed = state.reshape(3, group * rows, HD)
    attended = attend(packed[0], packed[1], packed[2], doc_lengths, first_row)
    state = attended.reshape((2,) * bits + (rows, HD))
    for step in reversed(range(bits)):
        axis_pos = bits - 1 - step
        bit_value = member // 2**step % 2
        retained = lax.dynamic_index_in_dim(state, bit_value, axis_pos, keepdims=False)
        leaving = lax.dynamic_index_in_dim(state, 1 - bit_value, axis_pos, keepdims=False)
        received = swapped(leaving, "seq", step)
        state = jnp.where(
            bit_value == 0,
            jnp.stack([retained, received], axis_pos),
            jnp.stack([received, retained], axis_pos),
        )
    return jnp.transpose(state.reshape(group, rows, HD), (1, 0, 2)).reshape(rows, width)


def solution(mesh):
    in_specs = (P("seq", "head"), P("seq", "head"), P("seq", "head"), P("seq"), P())
    out_specs = P("seq", "head")
    return jax.shard_map(body, mesh=mesh, in_specs=in_specs, out_specs=out_specs, check_vma=False)
```

profile of v0, /device:TPU:1, one launch (start us, length us, event | category | flops | bytes accessed | tf_op | source)
XLA Modules:
  0.0 235.5 jit_solution(10286477698136087776)
XLA Ops:
  0.0 0.7 add_select_fusion
  0.7 0.9 reduce-window.20
  1.6 0.2 slice_reduce_fusion
  2.0 2.9 %scatter_custom_fusion = s32[576]{0:T(1024)S(1)} fusion(s32[384]{0:T(512)S(1)} %compare_select_fusion.1, s32[384]{0:T(512)S(1)} %get-tuple-element.77, s32[]{:T(128)} %constant.151.clone.1), kind=kCustom, calls=%fused_computation.44 | custom fusion | bytes 2308 | tf_op jit(solution)/shard_map/scatter | solution.py:73
  4.9 0.7 all_to_all.9
  5.7 14.8 %all-to-all-start = ((s32[64,1,9]{2,1,0:T(1,128)}), s32[64,1,9]{2,1,0:T(1,128)S(1)}, u32[]{:S(2)}, u32[]{:S(2)}) async-start(s32[64,1,9]{2,1,0:T(1,128)} %bitcast.5), calls=%async_computation | async-start | bytes 65536 | tf_op jit(solution)/shard_map/all_to_all | solution.py:81
  20.5 1.4 maximum_bitcast_fusion
  21.9 1.0 copy.31
  22.9 2.0 broadcast_in_dim.42
  25.0 42.0 %scatter_fusion = bf16[3,576,512]{2,0,1:T(4,128)(2,1)} fusion(bf16[3,576,512]{2,0,1:T(4,128)(2,1)} %broadcast_in_dim.42, s32[384]{0:T(512)S(1)} %compare_select_fusion.1, bf16[384,3,512]{2,1,0:T(4,128)(2,1)S(1)} %copy.31), kind=kCustom, calls=%fused_computation.1 | custom fusion | bytes 3540480 | tf_op jit(solution)/shard_map/scatter | solution.py:72
  67.0 10.4 %all-to-all-start.1 = ((bf16[3,64,9,512]{3,0,2,1:T(4,128)(2,1)}), bf16[3,64,9,512]{3,0,2,1:T(4,128)(2,1)S(1)}, u32[]{:S(2)}, u32[]{:S(2)}) async-start(bf16[3,64,9,512]{3,0,2,1:T(4,128)(2,1)} %bitcast.10), calls=%async_computation.1 | async-start | bytes 4718592 | tf_op jit(solution)/shard_map/all_to_all | solution.py:74
  77.4 0.5 broadcast.76
  77.9 0.7 reduce.8
  78.8 53.7 %all-to-all-done.1 = bf16[3,64,9,512]{3,0,2,1:T(4,128)(2,1)S(1)} async-done(((bf16[3,64,9,512]{3,0,2,1:T(4,128)(2,1)}), bf16[3,64,9,512]{3,0,2,1:T(4,128)(2,1)S(1)}, u32[]{:S(2)}, u32[]{:S(2)}) %all-to-all-start.1) | async-done | bytes 1769504 | tf_op jit(solution)/shard_map/all_to_all | solution.py:74
  132.5 1.4 copy-done
  133.9 0.4 broadcast_in_dim.39
  134.3 47.4 %scatter_fusion.1 = bf16[3,385,512]{2,0,1:T(4,128)(2,1)S(1)} fusion(bf16[3,385,512]{2,0,1:T(4,128)(2,1)S(1)} %broadcast_in_dim.39, s32[576]{0:T(1024)S(1)} %fusion.24, bf16[576,3,512]{2,1,0:T(4,128)(2,1)} %bitcast.75), kind=kCustom, calls=%fused_computation.2 | custom fusion | bytes 5310720 | tf_op jit(solution)/shard_map/scatter | solution.py:85
  181.7 0.5 slice.28
  182.2 1.3 copy.32
  183.7 4.2 %collective-permute-start = (bf16[3,2,384,128]{2,3,1,0:T(8,128)(2,1)S(1)}, bf16[3,2,384,128]{2,3,1,0:T(8,128)(2,1)S(1)}, u32[]{:S(2)}, u32[]{:S(2)}) collective-permute-start(bf16[3,2,384,128]{2,3,1,0:T(8,128)(2,1)S(1)} %get-tuple-element.72), channel_id=1, source_target_pairs={{0,8},{8,0},{16,24},{24,16},{32,40},{40,32},{48,56},{56,48},{64,72... | collective-permute-start | bytes 1769480 | tf_op jit(solution)/shard_map/ppermute | solution.py:22
  187.9 1.6 collective-permute-done
  189.8 3.3 %collective-permute-start.1 = (bf16[3,2,384,128]{2,3,1,0:T(8,128)(2,1)S(1)}, bf16[3,2,384,128]{2,3,1,0:T(8,128)(2,1)S(1)}, u32[]{:S(2)}, u32[]{:S(2)}) collective-permute-start(bf16[3,2,384,128]{2,3,1,0:T(8,128)(2,1)S(1)} %get-tuple-element.70), channel_id=1, source_target_pairs={{0,16},{16,0},{8,24},{24,8},{32,48},{48,32},{40,56},{56,40},{64,80... | collective-permute-start | bytes 1769480 | tf_op jit(solution)/shard_map/ppermute | solution.py:22
  193.2 0.2 reduce-window.19
  193.5 0.5 convert_reduce_fusion
  194.0 12.2 %collective-permute-done.1 = bf16[3,2,384,128]{2,3,1,0:T(8,128)(2,1)S(1)} collective-permute-done((bf16[3,2,384,128]{2,3,1,0:T(8,128)(2,1)S(1)}, bf16[3,2,384,128]{2,3,1,0:T(8,128)(2,1)S(1)}, u32[]{:S(2)}, u32[]{:S(2)}) %collective-permute-start.1) | collective-permute-done | bytes 589856 | tf_op jit(solution)/shard_map/ppermute | solution.py:22
  206.2 0.2 maximum_select_fusion.1
  206.5 0.2 copy.33
  206.8 0.2 copy.34
  207.0 0.2 copy.35
  207.2 14.7 %while.10 = (s32[]{:T(128)}, bf16[3,512,128]{2,1,0:T(8,128)(2,1)S(1)}, s32[3]{0:T(128)S(1)}, s32[1536]{0:T(1024)S(1)}, s32[1536]{0:T(1024)S(1)}, /*index=5*/bf16...) while((s32[]{:T(128)}, ...), condition=%wide.region_11.12_spmd, body=%wide.region_8.11_spmd.sunk | while | flops 416939008 | bytes 10561727 | solution.py:51
  207.3 0.7 dynamic_slice.66
  208.8 1.0 fusion.41
  209.7 1.0 fusion.42
  210.7 1.4 fusion.43
  212.2 0.7 dynamic_slice.66
  213.7 1.0 fusion.41
  214.6 1.0 fusion.42
  215.6 1.4 fusion.43
  217.1 0.7 dynamic_slice.66
  218.6 1.0 fusion.41
  219.5 1.0 fusion.42
  220.5 1.4 fusion.43
  222.0 3.1 %collective-permute-start.2 = (bf16[2,384,128]{2,1,0:T(8,128)(2,1)S(1)}, bf16[2,384,128]{2,1,0:T(8,128)(2,1)S(1)}, u32[]{:S(2)}, u32[]{:S(2)}) collective-permute-start(bf16[2,384,128]{2,1,0:T(8,128)(2,1)S(1)} %get-tuple-element.76), channel_id=1, source_target_pairs={{0,16},{16,0},{8,24},{24,8},{32,48},{48,32},{40,56},{56,40},{64,80... | collective-permute-start | bytes 589832 | tf_op jit(solution)/shard_map/ppermute | solution.py:22
  225.1 4.0 %collective-permute-done.2 = bf16[2,384,128]{2,1,0:T(8,128)(2,1)S(1)} collective-permute-done((bf16[2,384,128]{2,1,0:T(8,128)(2,1)S(1)}, bf16[2,384,128]{2,1,0:T(8,128)(2,1)S(1)}, u32[]{:S(2)}, u32[]{:S(2)}) %collective-permute-start.2) | collective-permute-done | bytes 196640 | tf_op jit(solution)/shard_map/ppermute | solution.py:22
  229.2 4.0 %collective-permute-start.3 = (bf16[2,384,128]{2,1,0:T(8,128)(2,1)S(1)}, bf16[2,384,128]{2,1,0:T(8,128)(2,1)S(1)}, u32[]{:S(2)}, u32[]{:S(2)}) collective-permute-start(bf16[2,384,128]{2,1,0:T(8,128)(2,1)S(1)} %get-tuple-element.74), channel_id=1, source_target_pairs={{0,8},{8,0},{16,24},{24,16},{32,40},{40,32},{48,56},{56,48},{64,72... | collective-permute-start | bytes 589832 | tf_op jit(solution)/shard_map/ppermute | solution.py:22
  233.2 1.0 collective-permute-done.3
  234.3 0.4 copy.36
  234.7 0.8 copy.41
  (30 shorter events, 1.7 us)
Async XLA Ops:
  5.7 61.3 %all-to-all-start = ((s32[64,1,9]{2,1,0:T(1,128)}), s32[64,1,9]{2,1,0:T(1,128)S(1)}, u32[]{:S(2)}, u32[]{:S(2)}) async-start(s32[64,1,9]{2,1,0:T(1,128)} %bitcast.5), calls=%async_computation | async-start | bytes 65536 | tf_op jit(solution)/shard_map/all_to_all | solution.py:81
  67.0 65.5 %all-to-all-start.1 = ((bf16[3,64,9,512]{3,0,2,1:T(4,128)(2,1)}), bf16[3,64,9,512]{3,0,2,1:T(4,128)(2,1)S(1)}, u32[]{:S(2)}, u32[]{:S(2)}) async-start(bf16[3,64,9,512]{3,0,2,1:T(4,128)(2,1)} %bitcast.10), calls=%async_computation.1 | async-start | bytes 4718592 | tf_op jit(solution)/shard_map/all_to_all | solution.py:74
  132.5 1.4 copy-start
  183.7 5.8 %collective-permute-start = (bf16[3,2,384,128]{2,3,1,0:T(8,128)(2,1)S(1)}, bf16[3,2,384,128]{2,3,1,0:T(8,128)(2,1)S(1)}, u32[]{:S(2)}, u32[]{:S(2)}) collective-permute-start(bf16[3,2,384,128]{2,3,1,0:T(8,128)(2,1)S(1)} %get-tuple-element.72), channel_id=1, source_target_pairs={{0,8},{8,0},{16,24},{24,16},{32,40},{40,32},{48,56},{56,48},{64,72... | collective-permute-start | bytes 1769480 | tf_op jit(solution)/shard_map/ppermute | solution.py:22
  189.5 3.6 %copy-start.1 = (s32[128]{0:T(128)S(1)}, s32[128]{0:T(128)}, u32[]{:S(2)}) copy-start(s32[128]{0:T(128)} %param.11) | copy-start | bytes 1540
  189.8 16.4 %collective-permute-start.1 = (bf16[3,2,384,128]{2,3,1,0:T(8,128)(2,1)S(1)}, bf16[3,2,384,128]{2,3,1,0:T(8,128)(2,1)S(1)}, u32[]{:S(2)}, u32[]{:S(2)}) collective-permute-start(bf16[3,2,384,128]{2,3,1,0:T(8,128)(2,1)S(1)} %get-tuple-element.70), channel_id=1, source_target_pairs={{0,16},{16,0},{8,24},{24,8},{32,48},{48,32},{40,56},{56,40},{64,80... | collective-permute-start | bytes 1769480 | tf_op jit(solution)/shard_map/ppermute | solution.py:22
  222.0 7.1 %collective-permute-start.2 = (bf16[2,384,128]{2,1,0:T(8,128)(2,1)S(1)}, bf16[2,384,128]{2,1,0:T(8,128)(2,1)S(1)}, u32[]{:S(2)}, u32[]{:S(2)}) collective-permute-start(bf16[2,384,128]{2,1,0:T(8,128)(2,1)S(1)} %get-tuple-element.76), channel_id=1, source_target_pairs={{0,16},{16,0},{8,24},{24,8},{32,48},{48,32},{40,56},{56,40},{64,80... | collective-permute-start | bytes 589832 | tf_op jit(solution)/shard_map/ppermute | solution.py:22
  229.2 5.1 %collective-permute-start.3 = (bf16[2,384,128]{2,1,0:T(8,128)(2,1)S(1)}, bf16[2,384,128]{2,1,0:T(8,128)(2,1)S(1)}, u32[]{:S(2)}, u32[]{:S(2)}) collective-permute-start(bf16[2,384,128]{2,1,0:T(8,128)(2,1)S(1)} %get-tuple-element.74), channel_id=1, source_target_pairs={{0,8},{8,0},{16,24},{24,16},{32,40},{40,32},{48,56},{56,48},{64,72... | collective-permute-start | bytes 589832 | tf_op jit(solution)/shard_map/ppermute | solution.py:22
where the time goes:
time: 238 us; the launch traced here: 236 us
  local copies, waits for them, and re-layouts  106 us (45%)
  waiting for transfers between devices  72.5 us (30%)
  starting transfers between devices  39.8 us (17%)
  other arithmetic  8.02 us (3%)
  matrix products  7.16 us (3%)
    all_to_all x1, waiting for transfers between devices, body(): lax.all_to_all(outgoing.reshape(3, devices, capacity, width), 'seq', spli...  53.7 us
    scatter x1, local copies, waits for them, and re-layouts, body(): placed.at[:, arrived.reshape(-1)]  47.4 us
    scatter x1, local copies, waits for them, and re-layouts, body(): jnp.zeros((3, devices * capacity, width), jnp.bfloat16).at[:, slot]  42 us
    ppermute x4, waiting for transfers between devices, swapped(): return lax.ppermute(block, axis, route)  18.8 us
    all_to_all x1, starting transfers between devices, body(): lax.all_to_all(places.reshape(devices, capacity), 'seq', split_axis=0, co...  14.8 us
    ppermute x4, starting transfers between devices, swapped(): return lax.ppermute(block, axis, route)  14.6 us
    all_to_all x1, starting transfers between devices, body(): lax.all_to_all(outgoing.reshape(3, devices, capacity, width), 'seq', spli...  10.4 us
  transfers between devices with their start and end apart: 6, of which 5 were waited for; matrix products, arithmetic and copies ran while one was open for 21% of the time, Pallas kernels for 0%

commit v1 on v0

v1 whole, which is shorter than its diff:
```python
import functools
import math

import jax
import jax.numpy as jnp
from jax import lax
from jax.experimental import pallas as pl
from jax.experimental.pallas import tpu as pltpu
from jax.sharding import PartitionSpec as P

HD = 128
ROWS = 384
CAP = 9
CHIP = 2 * ROWS
NZ, NX = 8, 4
NEG = -1e30
MESH = pl.DeviceIdType.MESH
BF = jnp.bfloat16
F32 = jnp.float32
I32 = jnp.int32
WIDE = 7 * HD
NT = (((1,), (1,)), ((), ()))


def iota(shape, dim):
    return lax.broadcasted_iota(I32, shape, dim)


def kernel(q_ref, k_ref, v_ref, t_ref, len_ref, out_ref, send, recv, placed, bias, dense, mixed, send_sem, recv_sem, swap_send, swap_recv):
    me = lax.axis_index("seq")
    head = lax.axis_index("head")
    z, x, c = me // 8, (me // 2) % 4, me % 2

    def peer(k):
        rz, rx, xc = k // 8, (k // 2) % 4, k % 2
        return (((z + rz) % 8) * 8 + ((x + rx) % 4) * 2 + (c + xc) % 2, head)

    barrier = pltpu.get_barrier_semaphore()
    for k in range(1, 64):
        pl.semaphore_signal(barrier, inc=1, device_id=peer(k), device_id_type=MESH)

    t = t_ref[...]
    dev = jnp.floor((t.astype(F32) + 0.5) * (1.0 / ROWS)).astype(I32)
    local = t - dev * ROWS
    rzv = ((dev >> 3) - z) & 7
    rxv = (((dev >> 1) & 3) - x) & 3
    cc = dev & 1
    m = rzv * 4 + rxv
    flags = iota((64, ROWS), 0) == m * 2 + cc
    before = (iota((ROWS, ROWS), 0) < iota((ROWS, ROWS), 1)).astype(BF)
    cum = jnp.dot(flags.astype(F32).astype(BF), before, preferred_element_type=F32)
    rank = jnp.sum(jnp.where(flags, cum, 0.0), axis=0, keepdims=True).astype(I32)
    s = cc * CAP + rank
    place = cc * ROWS + local
    hi, lo = ((place >> 4) + 1).astype(F32), (place & 15).astype(F32)
    over = s >= 16
    main_row = jnp.where(over, -1, m * 16 + s)
    left_row = jnp.where(over, m * 16 + s - 16, -1000)
    place_row = m * 16 + jnp.where(over, 14, 12)
    lanes = iota((HD, ROWS), 0)
    hot = []
    for core in range(2):
        kk = rxv * 2 + ((c + core) & 1)
        main_hot = lanes == kk * 16 + s
        left_hot = ((lanes >> 4) == kk) & ((lanes & 15) < 12) & ((lanes & 1) == s - 16)
        hot.append(jnp.where(over, left_hot.astype(F32), main_hot.astype(F32)).astype(BF))
    hot = jnp.concatenate(hot, axis=0)

    copies = {}

    def build(chunk):
        rows = iota((256, ROWS), 0) + chunk * 256
        pick = (rows == main_row).astype(F32).astype(BF)
        at = pl.ds(chunk * 16, 16)
        left = lax.dot_general(
            (jnp.where(rows == place_row, hi, 0.0) + jnp.where(rows == place_row + 1, lo, 0.0)).astype(BF),
            hot, NT, preferred_element_type=F32)
        for a, ref in enumerate((q_ref, k_ref, v_ref)):
            got = jnp.dot(pick, ref[...], preferred_element_type=F32).astype(BF)
            for core in range(2):
                send[at, core, :, a * 256:(a + 1) * 256] = got[:, core * 256:(core + 1) * 256].reshape(16, 16, 256)
            for j in range(2):
                b = a * 2 + j
                pick_left = (rows - 2 * b == left_row).astype(F32).astype(BF)
                both = jnp.concatenate([ref[:, j * HD:(j + 1) * HD], ref[:, 256 + j * HD:256 + (j + 1) * HD]], axis=1)
                left = left + jnp.dot(pick_left, both, preferred_element_type=F32)
        left = left.astype(BF)
        for core in range(2):
            send[at, core, :, 768:896] = left[:, core * HD:(core + 1) * HD].reshape(16, 16, HD)

    def start(k):
        copy = pltpu.make_async_remote_copy(
            src_ref=send.at[k // 2, (c + k % 2) % 2], dst_ref=recv.at[k],
            send_sem=send_sem.at[k], recv_sem=recv_sem.at[k],
            device_id=peer(k), device_id_type=MESH)
        copy.start()
        copies[k] = copy

    order = (4, 3, 5, 2, 6, 1, 7, 0)
    build(1)
    pl.semaphore_wait(barrier, 63)
    for rz in (4, 5, 6, 7):
        for i in range(8):
            start(rz * 8 + i)
    build(0)
    for rz in (3, 2, 1, 0):
        for i in range(8):
            if rz * 8 + i > 0:
                start(rz * 8 + i)
    recv[0] = send[0, c]

    lens = jnp.broadcast_to(len_ref[...], (16, HD))
    earlier = (iota((HD, HD), 0) < iota((HD, HD), 1)).astype(BF)
    starts = (
        jnp.dot((lens >> 8).astype(F32).astype(BF), earlier, preferred_element_type=F32) * 256.0
        + jnp.dot((lens & 255).astype(F32).astype(BF), earlier, preferred_element_type=F32))[0:1]
    starts = starts - ((me // 2) * CHIP).astype(F32)

    def mask(i, carry):
        row = (iota((256, HD), 0) + i * 256).astype(F32)
        first = jnp.max(jnp.where(starts <= row, starts, -1e9), axis=1, keepdims=True)
        rows = (iota((256, CHIP), 0) + i * 256).astype(F32)
        cols = iota((256, CHIP), 1).astype(F32)
        bias[pl.ds(i * 256, 256), :] = jnp.where((cols <= rows) & (cols >= first), 0.0, NEG)
        return carry

    lax.fori_loop(0, 3, mask, 0)

    block = (iota((HD, HD), 0) & 15) >> 1
    groups = ((4, 5), (6, 7), (3, 2), (1, 0))
    for step, pair in enumerate(groups):
        places = []
        for g, rz in enumerate(pair):
            for i in range(8):
                if rz * 8 + i > 0:
                    copies[rz * 8 + i].wait_recv()
            tail = recv[rz * 8:(rz + 1) * 8, :, 768:896]
            total = jnp.sum(tail.astype(F32), axis=0)
            places.append(total[12:13] * 16.0 + total[13:14] - 16.0)
            places.append(total[14:15] * 16.0 + total[15:16] - 16.0)
            dense[g * 256:g * 256 + HD, :] = recv[rz * 8:(rz + 1) * 8, :, 0:768].reshape(HD, 768)
            tail = tail.reshape(HD, HD)
            for b in range(6):
                dense[g * 256 + HD:(g + 1) * 256, b * HD:(b + 1) * HD] = jnp.where(block == b, tail, jnp.zeros_like(tail))
        places = jnp.concatenate(places, axis=1).astype(I32)

        def deliver(i, carry, step=step, places=places):
            at = pl.ds(i * 256, 256)
            pick = (iota((256, 512), 0) + i * 256 == places).astype(F32).astype(BF)
            got = jnp.dot(pick, dense[...], preferred_element_type=F32).astype(BF)
            placed[at, :] = got if step == 0 else placed[at, :] + got
            return carry

        lax.fori_loop(0, 3, deliver, 0)

    scale = 1.0 / math.sqrt(HD)
    swaps = []
    for j in range(2):
        for i in range(3):
            upto = (i + 1) * 256
            at = slice(i * 256, upto)
            scores = lax.dot_general(
                placed[at, j * HD:(j + 1) * HD], placed[0:upto, 256 + j * HD:256 + (j + 1) * HD],
                NT, preferred_element_type=F32) * scale + bias[at, 0:upto]
            top = jnp.max(scores, axis=1, keepdims=True)
            weights = jnp.exp(scores - top)
            total = jnp.sum(weights, axis=1, keepdims=True)
            mix = jnp.dot(weights.astype(BF), placed[0:upto, 512 + j * HD:512 + (j + 1) * HD], preferred_element_type=F32)
            mixed[at, j * HD:(j + 1) * HD] = (mix / total).astype(BF)
        cols = pl.ds(pl.multiple_of(c * 256 + j * HD, HD), HD)
        swap = pltpu.make_async_remote_copy(
            src_ref=mixed.at[pl.ds(pl.multiple_of((1 - c) * ROWS, ROWS), ROWS), j * HD:(j + 1) * HD],
            dst_ref=out_ref.at[:, cols],
            send_sem=swap_send.at[j], recv_sem=swap_recv.at[j],
            device_id=peer(1), device_id_type=MESH)
        swap.start()
        swaps.append(swap)
        out_ref[:, cols] = mixed[pl.ds(pl.multiple_of(c * ROWS, ROWS), ROWS), j * HD:(j + 1) * HD]
    for copy in copies.values():
        copy.wait_send()
    for swap in swaps:
        swap.wait()


def body(queries, keys, values, target_row, doc_lengths):
    vmem = pl.BlockSpec(memory_space=pltpu.VMEM)
    return pl.pallas_call(
        kernel,
        out_shape=jax.ShapeDtypeStruct(queries.shape, BF),
        in_specs=[vmem] * 5,
        out_specs=vmem,
        scratch_shapes=[
            pltpu.VMEM((32, 2, 16, WIDE), BF),
            pltpu.VMEM((64, 16, WIDE), BF),
            pltpu.VMEM((CHIP, 768), BF),
            pltpu.VMEM((CHIP, CHIP), F32),
            pltpu.VMEM((512, 768), BF),
            pltpu.VMEM((CHIP, 256), BF),
            pltpu.SemaphoreType.DMA((64,)),
            pltpu.SemaphoreType.DMA((64,)),
            pltpu.SemaphoreType.DMA((2,)),
            pltpu.SemaphoreType.DMA((2,)),
        ],
        compiler_params=pltpu.CompilerParams(collective_id=0, has_side_effects=True, vmem_limit_bytes=40 * 2**20),
    )(queries, keys, values, target_row.reshape(1, -1), doc_lengths.reshape(1, -1))


def solution(mesh):
    in_specs = (P("seq", "head"), P("seq", "head"), P("seq", "head"), P("seq"), P())
    return jax.shard_map(body, mesh=mesh, in_specs=in_specs, out_specs=P("seq", "head"), check_vma=False)
```

time: 238 us -> 70.8 us (0.30)
  local copies, waits for them, and re-layouts: 106 us -> 4.43 us
  waiting for transfers between devices: 72.5 us -> 0 us
  Pallas kernels: 0 us -> 66.1 us
  starting transfers between devices: 39.8 us -> 0 us
  other arithmetic: 8.02 us -> 0 us
  matrix products: 7.16 us -> 0 us
    scatter x3 -> x0, local copies, waits for them, and re-layouts: 92.3 us -> none  [the longest x1 47.4 us: body(): placed.at[:, arrived.reshape(-1)]]
    pallas_call x0 -> x1, Pallas kernels: none -> 66.1 us  [body(): pl.pallas_call(kernel, out_shape=jax.ShapeDtypeStruct(queries.shape, BF),...]
    all_to_all x2 -> x0, waiting for transfers between devices: 53.7 us -> none  [the longest x1 53.7 us: body(): lax.all_to_all(outgoing.reshape(3, devices, capacity, width), 'seq', spli...]
    all_to_all x2 -> x0, starting transfers between devices: 25.2 us -> none  [the longest x1 14.8 us: body(): lax.all_to_all(places.reshape(devices, capacity), 'seq', split_axis=0, co...]
    ppermute x4 -> x0, waiting for transfers between devices: 18.8 us -> none  [swapped(): return lax.ppermute(block, axis, route)]
    ppermute x4 -> x0, starting transfers between devices: 14.6 us -> none  [swapped(): return lax.ppermute(block, axis, route)]
    dot_general x6 -> x0, matrix products: 7.16 us -> none  [the longest x3 4.28 us: one_block(): jnp.dot(weights.astype(jnp.bfloat16), value_all, preferred_element_type=j...]
    reduce_sum x5 -> x0, other arithmetic: 3.54 us -> none  [the longest x3 2.93 us: one_block(): total = jnp.sum(weights, axis=1, keepdims=True)]
  transfers between devices with their start and end apart: 6 -> 0, of which waited for: 5 -> 0; matrix products, arithmetic and copies ran while one was open for 21% -> 0% of each run, Pallas kernels for 0% -> 0%
where the time goes in v1:
time: 70.8 us; the launch traced here: 70.5 us
  Pallas kernels  66.1 us (93%)
  local copies, waits for them, and re-layouts  4.43 us (6%)
    pallas_call x1, Pallas kernels, body(): pl.pallas_call(kernel, out_shape=jax.ShapeDtypeStruct(queries.shape, BF),...  66.1 us
    unnamed x9, local copies, waits for them, and re-layouts  3.74 us

profile of v1, /device:TPU:1, one launch (start us, length us, event | category | flops | bytes accessed | tf_op | source)
XLA Modules:
  0.0 70.5 jit_solution(10943449702566931197)
XLA Ops:
  0.0 0.0 copy-start.3
  0.0 0.7 reshape.6.t_ref
  0.7 0.0 copy-done.3
  0.7 0.0 copy-start
  0.7 1.0 %copy-done = bf16[384,512]{1,0:T(8,128)(2,1)S(1)} copy-done((bf16[384,512]{1,0:T(8,128)(2,1)S(1)}, bf16[384,512]{1,0:T(8,128)(2,1)}, u32[]{:S(2)}) %copy-start) | copy-done | bytes 393240
  1.7 0.0 copy-start.1
  1.7 1.0 %copy-done.1 = bf16[384,512]{1,0:T(8,128)(2,1)S(1)} copy-done((bf16[384,512]{1,0:T(8,128)(2,1)S(1)}, bf16[384,512]{1,0:T(8,128)(2,1)}, u32[]{:S(2)}) %copy-start.1) | copy-done | bytes 393240
  2.7 0.0 copy-start.2
  2.7 1.0 %copy-done.2 = bf16[384,512]{1,0:T(8,128)(2,1)S(1)} copy-done((bf16[384,512]{1,0:T(8,128)(2,1)S(1)}, bf16[384,512]{1,0:T(8,128)(2,1)}, u32[]{:S(2)}) %copy-start.2) | copy-done | bytes 393240
  3.7 66.1 %shard_map.55 = bf16[384,512]{1,0:T(8,128)(2,1)S(1)} custom-call(bf16[384,512]{1,0:T(8,128)(2,1)S(1)} %copy-done, bf16[384,512]{1,0:T(8,128)(2,1)S(1)} %copy-done.1, bf16[384,512]{1,0:T(8,128)(2,1)S(1)} %copy-done.2, s32[1,384]{1,0:T(1,128)S(1)} %reshape.6.t_ref, s32[1,128]{1,0:T(1,128)S(1)} %bitcast.1), custom_call_target="tpu_custom_call" | custom-call | tf_op jit(solution)/shard_map/pallas_call | solution.py:187
  69.8 0.7 %copy.7 = bf16[384,512]{1,0:T(8,128)(2,1)} copy(bf16[384,512]{1,0:T(8,128)(2,1)S(1)} %shard_map.55) | data formatting | bytes 786432
Async XLA Ops:
  0.0 0.7 copy-start.3
  0.7 1.0 %copy-start = (bf16[384,512]{1,0:T(8,128)(2,1)S(1)}, bf16[384,512]{1,0:T(8,128)(2,1)}, u32[]{:S(2)}) copy-start(bf16[384,512]{1,0:T(8,128)(2,1)} %q_ref.1) | copy-start | bytes 1179652
  1.7 1.0 %copy-start.1 = (bf16[384,512]{1,0:T(8,128)(2,1)S(1)}, bf16[384,512]{1,0:T(8,128)(2,1)}, u32[]{:S(2)}) copy-start(bf16[384,512]{1,0:T(8,128)(2,1)} %k_ref.1) | copy-start | bytes 1179652
  2.7 1.0 %copy-start.2 = (bf16[384,512]{1,0:T(8,128)(2,1)S(1)}, bf16[384,512]{1,0:T(8,128)(2,1)}, u32[]{:S(2)}) copy-start(bf16[384,512]{1,0:T(8,128)(2,1)} %v_ref.1) | copy-start | bytes 1179652

commit v2 on v1

--- a/solution.py
+++ b/solution.py
@@ -19,6 +19,8 @@
 F32 = jnp.float32
 I32 = jnp.int32
 WIDE = 7 * HD
+SELF = 56
+Z_ORDER = (4, 3, 5, 2, 6, 1, 7, 0)
 NT = (((1,), (1,)), ((), ()))
 
 
@@ -26,23 +28,32 @@
     return lax.broadcasted_iota(I32, shape, dim)
 
 
-def kernel(q_ref, k_ref, v_ref, t_ref, len_ref, out_ref, send, recv, placed, bias, dense, mixed, send_sem, recv_sem, swap_send, swap_recv):
+def kernel(q_hbm, k_hbm, v_hbm, t_hbm, len_hbm, out_ref, q_ref, k_ref, v_ref, t_ref, len_ref, in_sem, send, recv, placed, bias, dense, mixed, send_sem, recv_sem, swap_send, swap_recv):
     me = lax.axis_index("seq")
     head = lax.axis_index("head")
     z, x, c = me // 8, (me // 2) % 4, me % 2
 
     def peer(k):
-        rz, rx, xc = k // 8, (k // 2) % 4, k % 2
+        rz, rx, xc = Z_ORDER[k // 8], (k // 2) % 4, k % 2
         return (((z + rz) % 8) * 8 + ((x + rx) % 4) * 2 + (c + xc) % 2, head)
 
+    pairs = ((t_hbm, t_ref), (q_hbm, q_ref), (k_hbm, k_ref), (v_hbm, v_ref), (len_hbm, len_ref))
+    fetch = [pltpu.make_async_copy(src, dst, in_sem.at[i]) for i, (src, dst) in enumerate(pairs)]
+    for copy in fetch:
+        copy.start()
+
     barrier = pltpu.get_barrier_semaphore()
-    for k in range(1, 64):
+    for k in range(64):
+        if k == SELF:
+            continue
         pl.semaphore_signal(barrier, inc=1, device_id=peer(k), device_id_type=MESH)
 
-    t = t_ref[...]
+    fetch[0].wait()
+    t = t_ref[...].reshape(1, ROWS)
     dev = jnp.floor((t.astype(F32) + 0.5) * (1.0 / ROWS)).astype(I32)
     local = t - dev * ROWS
-    rzv = ((dev >> 3) - z) & 7
+    away = 4 - (((dev >> 3) - z) & 7)
+    rzv = jnp.where(away > 0, 2 * away - 1, -2 * away)
     rxv = (((dev >> 1) & 3) - x) & 3
     cc = dev & 1
     m = rzv * 4 + rxv
@@ -66,6 +77,8 @@
         hot.append(jnp.where(over, left_hot.astype(F32), main_hot.astype(F32)).astype(BF))
     hot = jnp.concatenate(hot, axis=0)
 
+    for copy in fetch[1:]:
+        copy.wait()
     copies = {}
 
     def build(chunk):
@@ -96,20 +109,17 @@
         copy.start()
         copies[k] = copy
 
-    order = (4, 3, 5, 2, 6, 1, 7, 0)
+    build(0)
+    pl.semaphore_wait(barrier, 63)
+    for k in range(32):
+        start(k)
     build(1)
-    pl.semaphore_wait(barrier, 63)
-    for rz in (4, 5, 6, 7):
-        for i in range(8):
-            start(rz * 8 + i)
-    build(0)
-    for rz in (3, 2, 1, 0):
-        for i in range(8):
-            if rz * 8 + i > 0:
-                start(rz * 8 + i)
-    recv[0] = send[0, c]
-
-    lens = jnp.broadcast_to(len_ref[...], (16, HD))
+    for k in range(32, 64):
+        if k != SELF:
+            start(k)
+    recv[SELF] = send[SELF // 2, c]
+
+    lens = jnp.broadcast_to(len_ref[...].reshape(1, HD), (16, HD))
     earlier = (iota((HD, HD), 0) < iota((HD, HD), 1)).astype(BF)
     starts = (
         jnp.dot((lens >> 8).astype(F32).astype(BF), earlier, preferred_element_type=F32) * 256.0
@@ -127,12 +137,12 @@
     lax.fori_loop(0, 3, mask, 0)
 
     block = (iota((HD, HD), 0) & 15) >> 1
-    groups = ((4, 5), (6, 7), (3, 2), (1, 0))
+    groups = ((0, 1), (2, 3), (4, 5), (6, 7))
     for step, pair in enumerate(groups):
         places = []
         for g, rz in enumerate(pair):
             for i in range(8):
-                if rz * 8 + i > 0:
+                if rz * 8 + i != SELF:
                     copies[rz * 8 + i].wait_recv()
             tail = recv[rz * 8:(rz + 1) * 8, :, 768:896]
             total = jnp.sum(tail.astype(F32), axis=0)
@@ -172,7 +182,7 @@
             src_ref=mixed.at[pl.ds(pl.multiple_of((1 - c) * ROWS, ROWS), ROWS), j * HD:(j + 1) * HD],
             dst_ref=out_ref.at[:, cols],
             send_sem=swap_send.at[j], recv_sem=swap_recv.at[j],
-            device_id=peer(1), device_id_type=MESH)
+            device_id=peer(SELF + 1), device_id_type=MESH)
         swap.start()
         swaps.append(swap)
         out_ref[:, cols] = mixed[pl.ds(pl.multiple_of(c * ROWS, ROWS), ROWS), j * HD:(j + 1) * HD]
@@ -187,9 +197,15 @@
     return pl.pallas_call(
         kernel,
         out_shape=jax.ShapeDtypeStruct(queries.shape, BF),
-        in_specs=[vmem] * 5,
+        in_specs=[pl.BlockSpec(memory_space=pl.ANY)] * 5,
         out_specs=vmem,
         scratch_shapes=[
+            pltpu.VMEM(queries.shape, BF),
+            pltpu.VMEM(queries.shape, BF),
+            pltpu.VMEM(queries.shape, BF),
+            pltpu.VMEM((ROWS,), I32),
+            pltpu.VMEM((HD,), I32),
+            pltpu.SemaphoreType.DMA((5,)),
             pltpu.VMEM((32, 2, 16, WIDE), BF),
             pltpu.VMEM((64, 16, WIDE), BF),
             pltpu.VMEM((CHIP, 768), BF),
@@ -201,8 +217,8 @@
             pltpu.SemaphoreType.DMA((2,)),
             pltpu.SemaphoreType.DMA((2,)),
         ],
-        compiler_params=pltpu.CompilerParams(collective_id=0, has_side_effects=True, vmem_limit_bytes=40 * 2**20),
-    )(queries, keys, values, target_row.reshape(1, -1), doc_lengths.reshape(1, -1))
+        compiler_params=pltpu.CompilerParams(collective_id=0, has_side_effects=True, vmem_limit_bytes=535 * 2**20 // 10),
+    )(queries, keys, values, target_row, doc_lengths)
 
 
 def solution(mesh):

time: 70.8 us -> 65.5 us (0.925)
  Pallas kernels: 66.1 us -> 63.2 us
  local copies, waits for them, and re-layouts: 4.43 us -> 2.08 us
    pallas_call x1, Pallas kernels: 66.1 us -> 63.2 us  [body(): pl.pallas_call(kernel, out_shape=jax.ShapeDtypeStruct(queries.shape, BF),...]
    unnamed x9 -> x5, local copies, waits for them, and re-layouts: 3.74 us -> 2.08 us
where the time goes in v2:
time: 65.5 us; the launch traced here: 65.3 us
  Pallas kernels  63.2 us (96%)
  local copies, waits for them, and re-layouts  2.08 us (3%)
    pallas_call x1, Pallas kernels, body(): pl.pallas_call(kernel, out_shape=jax.ShapeDtypeStruct(queries.shape, BF),...  63.2 us
    unnamed x5, local copies, waits for them, and re-layouts  2.08 us

profile of v2, /device:TPU:1, one launch (start us, length us, event | category | flops | bytes accessed | tf_op | source)
XLA Modules:
  0.0 65.3 jit_solution(15166265939324079103)
XLA Ops:
  0.0 0.0 copy-start
  0.0 0.7 %copy-done = s32[384]{0:T(512)S(1)} copy-done((s32[384]{0:T(512)S(1)}, s32[384]{0:T(512)}, u32[]{:S(2)}) %copy-start) | copy-done | bytes 1560
  0.7 0.0 copy-start.1
  0.7 0.7 %copy-done.1 = s32[128]{0:T(128)S(1)} copy-done((s32[128]{0:T(128)S(1)}, s32[128]{0:T(128)}, u32[]{:S(2)}) %copy-start.1) | copy-done | bytes 536
  1.3 63.2 %shard_map.55 = bf16[384,512]{1,0:T(8,128)(2,1)S(1)} custom-call(bf16[384,512]{1,0:T(8,128)(2,1)} %q_hbm.1, bf16[384,512]{1,0:T(8,128)(2,1)} %k_hbm.1, bf16[384,512]{1,0:T(8,128)(2,1)} %v_hbm.1, s32[384]{0:T(512)S(1)} %copy-done, s32[128]{0:T(128)S(1)} %copy-done.1), custom_call_target="tpu_custom_call" | custom-call | tf_op jit(solution)/shard_map/pallas_call | solution.py:197
  64.5 0.7 %copy.7 = bf16[384,512]{1,0:T(8,128)(2,1)} copy(bf16[384,512]{1,0:T(8,128)(2,1)S(1)} %shard_map.55) | data formatting | bytes 786432
Async XLA Ops:
  0.0 0.7 %copy-start = (s32[384]{0:T(512)S(1)}, s32[384]{0:T(512)}, u32[]{:S(2)}) copy-start(s32[384]{0:T(512)} %t_hbm.1) | copy-start | bytes 4612
  0.7 0.7 %copy-start.1 = (s32[128]{0:T(128)S(1)}, s32[128]{0:T(128)}, u32[]{:S(2)}) copy-start(s32[128]{0:T(128)} %len_hbm.1) | copy-start | bytes 1540

commit v3 on v1

--- a/solution.py
+++ b/solution.py
@@ -19,6 +19,23 @@
 F32 = jnp.float32
 I32 = jnp.int32
 WIDE = 7 * HD
+
+
+def spread(zs, first=0, last=8):
+    return [(zz, i) for i in range(first, last) for zz in zs]
+
+
+def mixed_with(a, b):
+    short, long = sorted((a, b), key=len)
+    out = []
+    for n, each in enumerate(long):
+        out.append(each)
+        out += short[n * len(short) // len(long):(n + 1) * len(short) // len(long)]
+    return out
+
+
+LOW_SENDS = ([(zz, i) for zz in range(4) for i in range(8)], [(zz, i) for zz in range(4,8) for i in range(8)])
+HIGH_SENDS = (spread((0, 3, 1, 2), 0, 2), mixed_with(spread((0, 3, 1, 2), 2), spread((4, 7, 5, 6))))
 NT = (((1,), (1,)), ((), ()))
 
 
@@ -26,26 +43,43 @@
     return lax.broadcasted_iota(I32, shape, dim)
 
 
-def kernel(q_ref, k_ref, v_ref, t_ref, len_ref, out_ref, send, recv, placed, bias, dense, mixed, send_sem, recv_sem, swap_send, swap_recv):
+def kernel(q_hbm, k_hbm, v_hbm, t_ref, len_ref, out_ref, q_ref, k_ref, v_ref, in_sem, send, recv, placed, bias, dense, mixed, ready, send_sem, recv_sem, swap_send, swap_recv):
     me = lax.axis_index("seq")
     head = lax.axis_index("head")
     z, x, c = me // 8, (me // 2) % 4, me % 2
 
-    def peer(k):
-        rz, rx, xc = k // 8, (k // 2) % 4, k % 2
-        return (((z + rz) % 8) * 8 + ((x + rx) % 4) * 2 + (c + xc) % 2, head)
+    def device(zz, i):
+        return (zz * 8 + ((x + i // 2) % 4) * 2 + (c + i % 2) % 2, head)
+
+    pairs = ((q_hbm, q_ref), (k_hbm, k_ref), (v_hbm, v_ref))
+    fetch = [pltpu.make_async_copy(src, dst, in_sem.at[i]) for i, (src, dst) in enumerate(pairs)]
+    for copy in fetch:
+        copy.start()
 
     barrier = pltpu.get_barrier_semaphore()
-    for k in range(1, 64):
-        pl.semaphore_signal(barrier, inc=1, device_id=peer(k), device_id_type=MESH)
+    for i in range(1, 8):
+        pl.semaphore_signal(barrier, inc=1, device_id=device(z, i), device_id_type=MESH)
+    for zz in range(1, 8):
+
+        @pl.when(zz > z)
+        def _(zz=zz):
+            for i in range(8):
+                pl.semaphore_signal(barrier, inc=1, device_id=device(zz, i), device_id_type=MESH)
+
+    pl.semaphore_wait(barrier, z * 8 + 7)
+    for zz in range(7):
+
+        @pl.when(zz < z)
+        def _(zz=zz):
+            for i in range(8):
+                pl.semaphore_signal(ready.at[z], inc=1, device_id=device(zz, i), device_id_type=MESH)
 
     t = t_ref[...]
     dev = jnp.floor((t.astype(F32) + 0.5) * (1.0 / ROWS)).astype(I32)
     local = t - dev * ROWS
-    rzv = ((dev >> 3) - z) & 7
     rxv = (((dev >> 1) & 3) - x) & 3
     cc = dev & 1
-    m = rzv * 4 + rxv
+    m = (dev >> 3) * 4 + rxv
     flags = iota((64, ROWS), 0) == m * 2 + cc
     before = (iota((ROWS, ROWS), 0) < iota((ROWS, ROWS), 1)).astype(BF)
     cum = jnp.dot(flags.astype(F32).astype(BF), before, preferred_element_type=F32)
@@ -66,7 +100,8 @@
         hot.append(jnp.where(over, left_hot.astype(F32), main_hot.astype(F32)).astype(BF))
     hot = jnp.concatenate(hot, axis=0)
 
-    copies = {}
+    for copy in fetch:
+        copy.wait()
 
     def build(chunk):
         rows = iota((256, ROWS), 0) + chunk * 256
@@ -88,26 +123,43 @@
         for core in range(2):
             send[at, core, :, 768:896] = left[:, core * HD:(core + 1) * HD].reshape(16, 16, HD)
 
-    def start(k):
-        copy = pltpu.make_async_remote_copy(
-            src_ref=send.at[k // 2, (c + k % 2) % 2], dst_ref=recv.at[k],
-            send_sem=send_sem.at[k], recv_sem=recv_sem.at[k],
-            device_id=peer(k), device_id_type=MESH)
-        copy.start()
-        copies[k] = copy
-
-    order = (4, 3, 5, 2, 6, 1, 7, 0)
+    def copy_of(zz, i, slot):
+        return pltpu.make_async_remote_copy(
+            src_ref=send.at[zz * 4 + i // 2, (c + i % 2) % 2], dst_ref=recv.at[slot],
+            send_sem=send_sem.at[zz * 8 + i], recv_sem=recv_sem.at[slot],
+            device_id=device(zz, i), device_id_type=MESH)
+
+    def start(sends, greeted):
+        for zz, i in sends:
+            if zz > 0 and zz not in greeted:
+                greeted.add(zz)
+
+                @pl.when(zz > z)
+                def _(zz=zz):
+                    pl.semaphore_wait(ready.at[zz], 8)
+
+            if i > 0:
+                copy_of(zz, i, z * 8 + i).start()
+            else:
+
+                @pl.when(zz != z)
+                def _(zz=zz):
+                    copy_of(zz, 0, z * 8).start()
+
+    def send_part(part):
+        for near, sends in enumerate((LOW_SENDS, HIGH_SENDS)):
+
+            @pl.when((z >= 4) == (near == 1))
+            def _(near=near, sends=sends):
+                start(sends[part], met[near])
+
+    met = (set(), set())
+
+    build(0)
+    send_part(0)
     build(1)
-    pl.semaphore_wait(barrier, 63)
-    for rz in (4, 5, 6, 7):
-        for i in range(8):
-            start(rz * 8 + i)
-    build(0)
-    for rz in (3, 2, 1, 0):
-        for i in range(8):
-            if rz * 8 + i > 0:
-                start(rz * 8 + i)
-    recv[0] = send[0, c]
+    send_part(1)
+    recv[z * 8] = send[z * 4, c]
 
     lens = jnp.broadcast_to(len_ref[...], (16, HD))
     earlier = (iota((HD, HD), 0) < iota((HD, HD), 1)).astype(BF)
@@ -127,13 +179,16 @@
     lax.fori_loop(0, 3, mask, 0)
 
     block = (iota((HD, HD), 0) & 15) >> 1
-    groups = ((4, 5), (6, 7), (3, 2), (1, 0))
+    groups = ((0, 1), (2, 3), (4, 5), (6, 7))
     for step, pair in enumerate(groups):
         places = []
         for g, rz in enumerate(pair):
-            for i in range(8):
-                if rz * 8 + i > 0:
-                    copies[rz * 8 + i].wait_recv()
+            @pl.when(rz != z)
+            def _(rz=rz):
+                copy_of(rz, 0, rz * 8).wait_recv()
+
+            for i in range(1, 8):
+                copy_of(rz, i, rz * 8 + i).wait_recv()
             tail = recv[rz * 8:(rz + 1) * 8, :, 768:896]
             total = jnp.sum(tail.astype(F32), axis=0)
             places.append(total[12:13] * 16.0 + total[13:14] - 16.0)
@@ -172,12 +227,18 @@
             src_ref=mixed.at[pl.ds(pl.multiple_of((1 - c) * ROWS, ROWS), ROWS), j * HD:(j + 1) * HD],
             dst_ref=out_ref.at[:, cols],
             send_sem=swap_send.at[j], recv_sem=swap_recv.at[j],
-            device_id=peer(1), device_id_type=MESH)
+            device_id=device(z, 1), device_id_type=MESH)
         swap.start()
         swaps.append(swap)
         out_ref[:, cols] = mixed[pl.ds(pl.multiple_of(c * ROWS, ROWS), ROWS), j * HD:(j + 1) * HD]
-    for copy in copies.values():
-        copy.wait_send()
+    for zz in range(8):
+
+        @pl.when(zz != z)
+        def _(zz=zz):
+            copy_of(zz, 0, z * 8).wait_send()
+
+        for i in range(1, 8):
+            copy_of(zz, i, z * 8 + i).wait_send()
     for swap in swaps:
         swap.wait()
 
@@ -187,21 +248,26 @@
     return pl.pallas_call(
         kernel,
         out_shape=jax.ShapeDtypeStruct(queries.shape, BF),
-        in_specs=[vmem] * 5,
+        in_specs=[pl.BlockSpec(memory_space=pl.ANY)] * 3 + [vmem] * 2,
         out_specs=vmem,
         scratch_shapes=[
+            pltpu.VMEM(queries.shape, BF),
+            pltpu.VMEM(queries.shape, BF),
+            pltpu.VMEM(queries.shape, BF),
+            pltpu.SemaphoreType.DMA((3,)),
             pltpu.VMEM((32, 2, 16, WIDE), BF),
             pltpu.VMEM((64, 16, WIDE), BF),
             pltpu.VMEM((CHIP, 768), BF),
             pltpu.VMEM((CHIP, CHIP), F32),
             pltpu.VMEM((512, 768), BF),
             pltpu.VMEM((CHIP, 256), BF),
+            pltpu.SemaphoreType.REGULAR((8,)),
             pltpu.SemaphoreType.DMA((64,)),
             pltpu.SemaphoreType.DMA((64,)),
             pltpu.SemaphoreType.DMA((2,)),
             pltpu.SemaphoreType.DMA((2,)),
         ],
-        compiler_params=pltpu.CompilerParams(collective_id=0, has_side_effects=True, vmem_limit_bytes=40 * 2**20),
+        compiler_params=pltpu.CompilerParams(collective_id=0, has_side_effects=True, vmem_limit_bytes=535 * 2**20 // 10),
     )(queries, keys, values, target_row.reshape(1, -1), doc_lengths.reshape(1, -1))
 
 

time: 70.8 us -> 62.4 us (0.88)
  Pallas kernels: 66.1 us -> 60.8 us
  local copies, waits for them, and re-layouts: 4.43 us -> 1.45 us
    pallas_call x1, Pallas kernels: 66.1 us -> 60.8 us  [body(): pl.pallas_call(kernel, out_shape=jax.ShapeDtypeStruct(queries.shape, BF),...]
    unnamed x9 -> x3, local copies, waits for them, and re-layouts: 3.74 us -> 0.75 us
where the time goes in v3:
time: 62.4 us; the launch traced here: 62.2 us
  Pallas kernels  60.8 us (97%)
  local copies, waits for them, and re-layouts  1.45 us (2%)
    pallas_call x1, Pallas kernels, body(): pl.pallas_call(kernel, out_shape=jax.ShapeDtypeStruct(queries.shape, BF),...  60.8 us

profile of v3, /device:TPU:1, one launch (start us, length us, event | category | flops | bytes accessed | tf_op | source)
XLA Modules:
  0.0 62.2 jit_solution(17546781353621473620)
XLA Ops:
  0.0 0.0 copy-start
  0.0 0.7 %reshape.6.t_ref = s32[1,384]{1,0:T(1,128)S(1)} reshape(s32[384]{0:T(512)} %param.8) | data formatting | bytes 3072 | tf_op jit(solution)/shard_map/reshape | solution.py:271
  0.7 0.0 copy-done
  0.7 60.8 %shard_map.55 = bf16[384,512]{1,0:T(8,128)(2,1)S(1)} custom-call(bf16[384,512]{1,0:T(8,128)(2,1)} %q_hbm.1, bf16[384,512]{1,0:T(8,128)(2,1)} %k_hbm.1, bf16[384,512]{1,0:T(8,128)(2,1)} %v_hbm.1, s32[1,384]{1,0:T(1,128)S(1)} %reshape.6.t_ref, s32[1,128]{1,0:T(1,128)S(1)} %bitcast.1), custom_call_target="tpu_custom_call" | custom-call | tf_op jit(solution)/shard_map/pallas_call | solution.py:248
  61.5 0.7 %copy.7 = bf16[384,512]{1,0:T(8,128)(2,1)} copy(bf16[384,512]{1,0:T(8,128)(2,1)S(1)} %shard_map.55) | data formatting | bytes 786432
Async XLA Ops:
  0.0 0.7 %copy-start = (s32[128]{0:T(128)S(1)}, s32[128]{0:T(128)}, u32[]{:S(2)}) copy-start(s32[128]{0:T(128)} %param.9) | copy-start | bytes 1540

commit v4 on v3

--- a/solution.py
+++ b/solution.py
@@ -65,14 +65,6 @@
         def _(zz=zz):
             for i in range(8):
                 pl.semaphore_signal(barrier, inc=1, device_id=device(zz, i), device_id_type=MESH)
-
-    pl.semaphore_wait(barrier, z * 8 + 7)
-    for zz in range(7):
-
-        @pl.when(zz < z)
-        def _(zz=zz):
-            for i in range(8):
-                pl.semaphore_signal(ready.at[z], inc=1, device_id=device(zz, i), device_id_type=MESH)
 
     t = t_ref[...]
     dev = jnp.floor((t.astype(F32) + 0.5) * (1.0 / ROWS)).astype(I32)
@@ -91,10 +83,18 @@
     main_row = jnp.where(over, -1, m * 16 + s)
     left_row = jnp.where(over, m * 16 + s - 16, -1000)
     place_row = m * 16 + jnp.where(over, 14, 12)
+    pl.semaphore_wait(barrier, z * 8 + 7)
+    for zz in range(7):
+
+        @pl.when(zz < z)
+        def _(zz=zz):
+            pl.semaphore_signal(ready.at[z], inc=1, device_id=device(zz, 0), device_id_type=MESH)
+
     lanes = iota((HD, ROWS), 0)
     hot = []
     for core in range(2):
         kk = rxv * 2 + ((c + core) & 1)
+        kk = (kk & 3) + 4 * (z % 2)
         main_hot = lanes == kk * 16 + s
         left_hot = ((lanes >> 4) == kk) & ((lanes & 15) < 12) & ((lanes & 1) == s - 16)
         hot.append(jnp.where(over, left_hot.astype(F32), main_hot.astype(F32)).astype(BF))
@@ -136,7 +136,7 @@
 
                 @pl.when(zz > z)
                 def _(zz=zz):
-                    pl.semaphore_wait(ready.at[zz], 8)
+                    pl.semaphore_wait(ready.at[zz], 1)
 
             if i > 0:
                 copy_of(zz, i, z * 8 + i).start()
@@ -178,25 +178,34 @@
 
     lax.fori_loop(0, 3, mask, 0)
 
-    block = (iota((HD, HD), 0) & 15) >> 1
-    groups = ((0, 1), (2, 3), (4, 5), (6, 7))
-    for step, pair in enumerate(groups):
+    block = (iota((64, HD), 0) & 15) >> 1
+    for step in range(4):
         places = []
-        for g, rz in enumerate(pair):
-            @pl.when(rz != z)
-            def _(rz=rz):
-                copy_of(rz, 0, rz * 8).wait_recv()
-
-            for i in range(1, 8):
-                copy_of(rz, i, rz * 8 + i).wait_recv()
-            tail = recv[rz * 8:(rz + 1) * 8, :, 768:896]
-            total = jnp.sum(tail.astype(F32), axis=0)
+        for g in range(2):
+            total = None
+            for odd in range(2):
+                zz = step // 2 * 4 + g * 2 + odd
+                first = zz * 8 + step % 2 * 4
+                for i in range(step % 2 * 4, step % 2 * 4 + 4):
+                    if i > 0:
+                        copy_of(zz, i, zz * 8 + i).wait_recv()
+                    else:
+
+                        @pl.when(zz != z)
+                        def _(zz=zz):
+                            copy_of(zz, 0, zz * 8).wait_recv()
+
+                at = slice(g * 256 + odd * 64, g * 256 + odd * 64 + 64)
+                at_left = slice(g * 256 + HD + odd * 64, g * 256 + HD + odd * 64 + 64)
+                tail = recv[first:first + 4, :, 768:896]
+                part = jnp.sum(tail.astype(F32), axis=0)
+                total = part if total is None else total + part
+                dense[at, :] = recv[first:first + 4, :, 0:768].reshape(64, 768)
+                tail = tail.reshape(64, HD)
+                for b in range(6):
+                    dense[at_left, b * HD:(b + 1) * HD] = jnp.where(block == b, tail, jnp.zeros_like(tail))
             places.append(total[12:13] * 16.0 + total[13:14] - 16.0)
             places.append(total[14:15] * 16.0 + total[15:16] - 16.0)
-            dense[g * 256:g * 256 + HD, :] = recv[rz * 8:(rz + 1) * 8, :, 0:768].reshape(HD, 768)
-            tail = tail.reshape(HD, HD)
-            for b in range(6):
-                dense[g * 256 + HD:(g + 1) * 256, b * HD:(b + 1) * HD] = jnp.where(block == b, tail, jnp.zeros_like(tail))
         places = jnp.concatenate(places, axis=1).astype(I32)
 
         def deliver(i, carry, step=step, places=places):

time: 62.4 us -> 61.7 us (0.989)
  Pallas kernels: 60.8 us -> 60.1 us
    pallas_call x1, Pallas kernels: 60.8 us -> 60.1 us  [body(): pl.pallas_call(kernel, out_shape=jax.ShapeDtypeStruct(queries.shape, BF),...]
where the time goes in v4:
time: 61.7 us; the launch traced here: 61.6 us
  Pallas kernels  60.1 us (97%)
  local copies, waits for them, and re-layouts  1.45 us (2%)
    pallas_call x1, Pallas kernels, body(): pl.pallas_call(kernel, out_shape=jax.ShapeDtypeStruct(queries.shape, BF),...  60.1 us

profile of v4, /device:TPU:1, one launch (start us, length us, event | category | flops | bytes accessed | tf_op | source)
XLA Modules:
  0.0 61.6 jit_solution(11871063501447357876)
XLA Ops:
  0.0 0.0 copy-start
  0.0 0.7 %reshape.6.t_ref = s32[1,384]{1,0:T(1,128)S(1)} reshape(s32[384]{0:T(512)} %param.8) | data formatting | bytes 3072 | tf_op jit(solution)/shard_map/reshape | solution.py:280
  0.7 0.0 copy-done
  0.7 60.1 %shard_map.55 = bf16[384,512]{1,0:T(8,128)(2,1)S(1)} custom-call(bf16[384,512]{1,0:T(8,128)(2,1)} %q_hbm.1, bf16[384,512]{1,0:T(8,128)(2,1)} %k_hbm.1, bf16[384,512]{1,0:T(8,128)(2,1)} %v_hbm.1, s32[1,384]{1,0:T(1,128)S(1)} %reshape.6.t_ref, s32[1,128]{1,0:T(1,128)S(1)} %bitcast.1), custom_call_target="tpu_custom_call" | custom-call | tf_op jit(solution)/shard_map/pallas_call | solution.py:257
  60.8 0.7 %copy.7 = bf16[384,512]{1,0:T(8,128)(2,1)} copy(bf16[384,512]{1,0:T(8,128)(2,1)S(1)} %shard_map.55) | data formatting | bytes 786432
Async XLA Ops:
  0.0 0.7 %copy-start = (s32[128]{0:T(128)S(1)}, s32[128]{0:T(128)}, u32[]{:S(2)}) copy-start(s32[128]{0:T(128)} %param.9) | copy-start | bytes 1540

commit v5 on v4

--- a/solution.py
+++ b/solution.py
@@ -215,31 +215,35 @@
             placed[at, :] = got if step == 0 else placed[at, :] + got
             return carry
 
-        lax.fori_loop(0, 3, deliver, 0)
+        lax.fori_loop(0, 3, deliver, 0, unroll=True)
 
     scale = 1.0 / math.sqrt(HD)
-    swaps = []
-    for j in range(2):
-        for i in range(3):
-            upto = (i + 1) * 256
-            at = slice(i * 256, upto)
+
+    def attend(half, dst, dst_rows):
+        upto = (half + 1) * ROWS
+        rows = slice(half * ROWS, upto)
+        for j in range(2):
             scores = lax.dot_general(
-                placed[at, j * HD:(j + 1) * HD], placed[0:upto, 256 + j * HD:256 + (j + 1) * HD],
-                NT, preferred_element_type=F32) * scale + bias[at, 0:upto]
+                placed[rows, j * HD:(j + 1) * HD], placed[0:upto, 256 + j * HD:256 + (j + 1) * HD],
+                NT, preferred_element_type=F32) * scale + bias[rows, 0:upto]
             top = jnp.max(scores, axis=1, keepdims=True)
             weights = jnp.exp(scores - top)
             total = jnp.sum(weights, axis=1, keepdims=True)
             mix = jnp.dot(weights.astype(BF), placed[0:upto, 512 + j * HD:512 + (j + 1) * HD], preferred_element_type=F32)
-            mixed[at, j * HD:(j + 1) * HD] = (mix / total).astype(BF)
-        cols = pl.ds(pl.multiple_of(c * 256 + j * HD, HD), HD)
-        swap = pltpu.make_async_remote_copy(
-            src_ref=mixed.at[pl.ds(pl.multiple_of((1 - c) * ROWS, ROWS), ROWS), j * HD:(j + 1) * HD],
-            dst_ref=out_ref.at[:, cols],
-            send_sem=swap_send.at[j], recv_sem=swap_recv.at[j],
-            device_id=device(z, 1), device_id_type=MESH)
-        swap.start()
-        swaps.append(swap)
-        out_ref[:, cols] = mixed[pl.ds(pl.multiple_of(c * ROWS, ROWS), ROWS), j * HD:(j + 1) * HD]
+            dst[:, dst_rows + j * HD:dst_rows + (j + 1) * HD] = (mix / total).astype(BF)
+
+    cols = pl.ds(pl.multiple_of(c * 256, 256), 256)
+    swap = pltpu.make_async_remote_copy(
+        src_ref=mixed, dst_ref=out_ref.at[:, cols], send_sem=swap_send, recv_sem=swap_recv,
+        device_id=device(z, 1), device_id_type=MESH)
+    for core in range(2):
+
+        @pl.when(c == core)
+        def _(core=core):
+            attend(1 - core, mixed, 0)
+            swap.start()
+            attend(core, out_ref, core * 256)
+
     for zz in range(8):
 
         @pl.when(zz != z)
@@ -248,8 +252,7 @@
 
         for i in range(1, 8):
             copy_of(zz, i, z * 8 + i).wait_send()
-    for swap in swaps:
-        swap.wait()
+    swap.wait()
 
 
 def body(queries, keys, values, target_row, doc_lengths):
@@ -269,12 +272,12 @@
             pltpu.VMEM((CHIP, 768), BF),
             pltpu.VMEM((CHIP, CHIP), F32),
             pltpu.VMEM((512, 768), BF),
-            pltpu.VMEM((CHIP, 256), BF),
+            pltpu.VMEM((ROWS, 256), BF),
             pltpu.SemaphoreType.REGULAR((8,)),
             pltpu.SemaphoreType.DMA((64,)),
             pltpu.SemaphoreType.DMA((64,)),
-            pltpu.SemaphoreType.DMA((2,)),
-            pltpu.SemaphoreType.DMA((2,)),
+            pltpu.SemaphoreType.DMA,
+            pltpu.SemaphoreType.DMA,
         ],
         compiler_params=pltpu.CompilerParams(collective_id=0, has_side_effects=True, vmem_limit_bytes=535 * 2**20 // 10),
     )(queries, keys, values, target_row.reshape(1, -1), doc_lengths.reshape(1, -1))

time: 61.7 us -> 60.2 us (0.976)
  Pallas kernels: 60.1 us -> 58.6 us
    pallas_call x1, Pallas kernels: 60.1 us -> 58.6 us  [body(): pl.pallas_call(kernel, out_shape=jax.ShapeDtypeStruct(queries.shape, BF),...]
where the time goes in v5:
time: 60.2 us; the launch traced here: 60 us
  Pallas kernels  58.6 us (97%)
  local copies, waits for them, and re-layouts  1.45 us (2%)
    pallas_call x1, Pallas kernels, body(): pl.pallas_call(kernel, out_shape=jax.ShapeDtypeStruct(queries.shape, BF),...  58.6 us

profile of v5, /device:TPU:1, one launch (start us, length us, event | category | flops | bytes accessed | tf_op | source)
XLA Modules:
  0.0 60.0 jit_solution(15781860424124178001)
XLA Ops:
  0.0 0.0 copy-start
  0.0 0.7 %reshape.6.t_ref = s32[1,384]{1,0:T(1,128)S(1)} reshape(s32[384]{0:T(512)} %param.8) | data formatting | bytes 3072 | tf_op jit(solution)/shard_map/reshape | solution.py:283
  0.7 0.0 copy-done
  0.7 58.6 %shard_map.55 = bf16[384,512]{1,0:T(8,128)(2,1)S(1)} custom-call(bf16[384,512]{1,0:T(8,128)(2,1)} %q_hbm.1, bf16[384,512]{1,0:T(8,128)(2,1)} %k_hbm.1, bf16[384,512]{1,0:T(8,128)(2,1)} %v_hbm.1, s32[1,384]{1,0:T(1,128)S(1)} %reshape.6.t_ref, s32[1,128]{1,0:T(1,128)S(1)} %bitcast.1), custom_call_target="tpu_custom_call" | custom-call | tf_op jit(solution)/shard_map/pallas_call | solution.py:260
  59.3 0.7 %copy.7 = bf16[384,512]{1,0:T(8,128)(2,1)} copy(bf16[384,512]{1,0:T(8,128)(2,1)S(1)} %shard_map.55) | data formatting | bytes 786432
Async XLA Ops:
  0.0 0.7 %copy-start = (s32[128]{0:T(128)S(1)}, s32[128]{0:T(128)}, u32[]{:S(2)}) copy-start(s32[128]{0:T(128)} %param.9) | copy-start | bytes 1540

commit v6 on v5

--- a/solution.py
+++ b/solution.py
@@ -34,8 +34,12 @@
     return out
 
 
-LOW_SENDS = ([(zz, i) for zz in range(4) for i in range(8)], [(zz, i) for zz in range(4,8) for i in range(8)])
-HIGH_SENDS = (spread((0, 3, 1, 2), 0, 2), mixed_with(spread((0, 3, 1, 2), 2), spread((4, 7, 5, 6))))
+LOW_SENDS = tuple([(zz, i) for zz in zs for i in range(8)] for zs in ((0, 1), (2, 3), (4, 5, 6, 7)))
+HIGH_SENDS = (
+    spread((0, 1), 0, 2),
+    spread((3, 2), 0, 2),
+    mixed_with(spread((0, 3, 1, 2), 2), spread((4, 7, 5, 6))),
+)
 NT = (((1,), (1,)), ((), ()))
 
 
@@ -104,16 +108,16 @@
         copy.wait()
 
     def build(chunk):
-        rows = iota((256, ROWS), 0) + chunk * 256
+        rows = iota((128, ROWS), 0) + chunk * 128
         pick = (rows == main_row).astype(F32).astype(BF)
-        at = pl.ds(chunk * 16, 16)
+        at = pl.ds(chunk * 8, 8)
         left = lax.dot_general(
             (jnp.where(rows == place_row, hi, 0.0) + jnp.where(rows == place_row + 1, lo, 0.0)).astype(BF),
             hot, NT, preferred_element_type=F32)
         for a, ref in enumerate((q_ref, k_ref, v_ref)):
             got = jnp.dot(pick, ref[...], preferred_element_type=F32).astype(BF)
             for core in range(2):
-                send[at, core, :, a * 256:(a + 1) * 256] = got[:, core * 256:(core + 1) * 256].reshape(16, 16, 256)
+                send[at, core, :, a * 256:(a + 1) * 256] = got[:, core * 256:(core + 1) * 256].reshape(8, 16, 256)
             for j in range(2):
                 b = a * 2 + j
                 pick_left = (rows - 2 * b == left_row).astype(F32).astype(BF)
@@ -121,7 +125,7 @@
                 left = left + jnp.dot(pick_left, both, preferred_element_type=F32)
         left = left.astype(BF)
         for core in range(2):
-            send[at, core, :, 768:896] = left[:, core * HD:(core + 1) * HD].reshape(16, 16, HD)
+            send[at, core, :, 768:896] = left[:, core * HD:(core + 1) * HD].reshape(8, 16, HD)
 
     def copy_of(zz, i, slot):
         return pltpu.make_async_remote_copy(
@@ -159,6 +163,9 @@
     send_part(0)
     build(1)
     send_part(1)
+    build(2)
+    build(3)
+    send_part(2)
     recv[z * 8] = send[z * 4, c]
 
     lens = jnp.broadcast_to(len_ref[...], (16, HD))

time: 60.2 us -> 59.8 us (level)
  no operation moved by 1% of the time
where the time goes in v6:
time: 59.8 us; the launch traced here: 59.6 us
  Pallas kernels  58.2 us (97%)
  local copies, waits for them, and re-layouts  1.45 us (2%)
    pallas_call x1, Pallas kernels, body(): pl.pallas_call(kernel, out_shape=jax.ShapeDtypeStruct(queries.shape, BF),...  58.2 us

profile of v6, /device:TPU:1, one launch (start us, length us, event | category | flops | bytes accessed | tf_op | source)
XLA Modules:
  0.0 59.6 jit_solution(9159651889286347246)
XLA Ops:
  0.0 0.0 copy-start
  0.0 0.7 %reshape.6.t_ref = s32[1,384]{1,0:T(1,128)S(1)} reshape(s32[384]{0:T(512)} %param.8) | data formatting | bytes 3072 | tf_op jit(solution)/shard_map/reshape | solution.py:290
  0.7 0.0 copy-done
  0.7 58.2 %shard_map.55 = bf16[384,512]{1,0:T(8,128)(2,1)S(1)} custom-call(bf16[384,512]{1,0:T(8,128)(2,1)} %q_hbm.1, bf16[384,512]{1,0:T(8,128)(2,1)} %k_hbm.1, bf16[384,512]{1,0:T(8,128)(2,1)} %v_hbm.1, s32[1,384]{1,0:T(1,128)S(1)} %reshape.6.t_ref, s32[1,128]{1,0:T(1,128)S(1)} %bitcast.1), custom_call_target="tpu_custom_call" | custom-call | tf_op jit(solution)/shard_map/pallas_call | solution.py:267
  58.9 0.7 %copy.7 = bf16[384,512]{1,0:T(8,128)(2,1)} copy(bf16[384,512]{1,0:T(8,128)(2,1)S(1)} %shard_map.55) | data formatting | bytes 786432
Async XLA Ops:
  0.0 0.7 %copy-start = (s32[128]{0:T(128)S(1)}, s32[128]{0:T(128)}, u32[]{:S(2)}) copy-start(s32[128]{0:T(128)} %param.9) | copy-start | bytes 1540

commit v7 on v6

--- a/solution.py
+++ b/solution.py
@@ -25,20 +25,11 @@
     return [(zz, i) for i in range(first, last) for zz in zs]
 
 
-def mixed_with(a, b):
-    short, long = sorted((a, b), key=len)
-    out = []
-    for n, each in enumerate(long):
-        out.append(each)
-        out += short[n * len(short) // len(long):(n + 1) * len(short) // len(long)]
-    return out
-
-
 LOW_SENDS = tuple([(zz, i) for zz in zs for i in range(8)] for zs in ((0, 1), (2, 3), (4, 5, 6, 7)))
 HIGH_SENDS = (
     spread((0, 1), 0, 2),
     spread((3, 2), 0, 2),
-    mixed_with(spread((0, 3, 1, 2), 2), spread((4, 7, 5, 6))),
+    spread((0, 3, 1, 2), 2) + spread((4, 7, 5, 6)),
 )
 NT = (((1,), (1,)), ((), ()))
 

time: 59.8 us -> 60.3 us (level)
  no operation moved by 1% of the time
where the time goes in v7:
time: 60.3 us; the launch traced here: 60.2 us
  Pallas kernels  58.7 us (97%)
  local copies, waits for them, and re-layouts  1.45 us (2%)
    pallas_call x1, Pallas kernels, body(): pl.pallas_call(kernel, out_shape=jax.ShapeDtypeStruct(queries.shape, BF),...  58.7 us

profile of v7, /device:TPU:1, one launch (start us, length us, event | category | flops | bytes accessed | tf_op | source)
XLA Modules:
  0.0 60.2 jit_solution(12874510151952756869)
XLA Ops:
  0.0 0.0 copy-start
  0.0 0.7 %reshape.6.t_ref = s32[1,384]{1,0:T(1,128)S(1)} reshape(s32[384]{0:T(512)} %param.8) | data formatting | bytes 3072 | tf_op jit(solution)/shard_map/reshape | solution.py:281
  0.7 0.0 copy-done
  0.7 58.7 %shard_map.55 = bf16[384,512]{1,0:T(8,128)(2,1)S(1)} custom-call(bf16[384,512]{1,0:T(8,128)(2,1)} %q_hbm.1, bf16[384,512]{1,0:T(8,128)(2,1)} %k_hbm.1, bf16[384,512]{1,0:T(8,128)(2,1)} %v_hbm.1, s32[1,384]{1,0:T(1,128)S(1)} %reshape.6.t_ref, s32[1,128]{1,0:T(1,128)S(1)} %bitcast.1), custom_call_target="tpu_custom_call" | custom-call | tf_op jit(solution)/shard_map/pallas_call | solution.py:258
  59.4 0.7 %copy.7 = bf16[384,512]{1,0:T(8,128)(2,1)} copy(bf16[384,512]{1,0:T(8,128)(2,1)S(1)} %shard_map.55) | data formatting | bytes 786432
Async XLA Ops:
  0.0 0.7 %copy-start = (s32[128]{0:T(128)S(1)}, s32[128]{0:T(128)}, u32[]{:S(2)}) copy-start(s32[128]{0:T(128)} %param.9) | copy-start | bytes 1540
